TPU v7x, 128 devices: a whole 4x4x4 slice. The times are simulated.
128 devices in a mesh: pipe: 2 (over core), dp: 32 (over x_hi, z, y), seq: 2 (over x_lo).
Axes of the slice: x: 4 (x_hi: 2, x_lo: 2; x = x_hi * 2 + x_lo), y: 4, z: 4, core: 2. Of those that a mesh axis runs over, the one named last changes fastest.
Arguments:
- activations: float32 [4, 32768, 256], P(None, ('dp', 'seq')), may hold values from -6 to 6
- cotangent: float32 [4, 32768, 256], P(None, ('dp', 'seq')), may hold values from -6 to 6
- cell_lengths: int32 [4, 32, 3], P(None, 'dp'), may hold values from 0 to 1023, as said below
- w_qkv: float32 [2, 256, 768], P('pipe'), may hold values from -0.375 to 0.375
- b_qv: float32 [2, 512], P('pipe'), may hold values from -3 to 3
- w_out: float32 [2, 256, 256], P('pipe'), may hold values from -1.5 to 1.5
- b_out: float32 [2, 256], P('pipe'), may hold values from -3 to 3
- gain_one: float32 [2, 256], P('pipe'), may hold values from 0.5 to 1.5
- shift_one: float32 [2, 256], P('pipe'), may hold values from -3 to 3
- w_in: float32 [2, 256, 512], P('pipe'), may hold values from -0.375 to 0.375
- b_in: float32 [2, 512], P('pipe'), may hold values from -3 to 3
- w_back: float32 [2, 512, 256], P('pipe'), may hold values from -0.25 to 0.25
- b_back: float32 [2, 256], P('pipe'), may hold values from -3 to 3
- gain_two: float32 [2, 256], P('pipe'), may hold values from 0.5 to 1.5
- shift_two: float32 [2, 256], P('pipe'), may hold values from -3 to 3
Outputs:
- final_output: float32 [4, 32768, 256], P('pipe', ('dp', 'seq'))
- input_grad: float32 [4, 32768, 256], P('pipe', ('dp', 'seq'))
- grad_w_qkv: float32 [2, 256, 768], P('pipe')
- grad_b_qv: float32 [2, 512], P('pipe')
- grad_w_out: float32 [2, 256, 256], P('pipe')
- grad_b_out: float32 [2, 256], P('pipe')
- grad_gain_one: float32 [2, 256], P('pipe')
- grad_shift_one: float32 [2, 256], P('pipe')
- grad_w_in: float32 [2, 256, 512], P('pipe')
- grad_b_in: float32 [2, 512], P('pipe')
- grad_w_back: float32 [2, 512, 256], P('pipe')
- grad_b_back: float32 [2, 256], P('pipe')
- grad_gain_two: float32 [2, 256], P('pipe')
- grad_shift_two: float32 [2, 256], P('pipe')
Inputs may be any that keep to these rules, and one draw needn't show every extreme that they name: cell_lengths[m, g] lists three cells packed from the start of group g's slot of micro-batch m: the first has 1 to 256 tokens, the last 0 to 256, the middle one the rest, and the middle one always covers place 512 of the slot. Together they fill 512 + 512 // 8 to 1024 places. In every micro-batch one group fills exactly 1024 places with a middle cell of 1023 tokens and an empty last cell.
All inputs are finite; a program needn't handle non-finite values.
Results may differ from a plain program's by a relative error of at most 0.0003.
Values sent between devices are 32-bit elements; how exact they have to be, the bound alone decides.
A program may use at most 256 MiB of HBM per device.

v0:
```python
import math

import jax
import jax.numpy as jnp
from jax import lax
from jax.sharding import PartitionSpec as P

HEADS = 4


PRECISE = lax.Precision.HIGHEST
EPSILON = 1e-06
NEGATIVE = -1e30


def from_behind(block, axis, distance):
    devices = range(lax.axis_size(axis))
    route = [((i - distance) % len(devices), i) for i in devices]
    return lax.ppermute(block, axis, route)


def layer_norm(values, gain_vector, bias_vector):
    center = values - jnp.mean(values, axis=-1, keepdims=True)
    spread = jnp.mean(center * center, axis=-1, keepdims=True)
    return center * lax.rsqrt(spread + EPSILON) * gain_vector + bias_vector


def segments(positions, cell_ends):
    return jnp.sum((positions[:, None] >= cell_ends[None, :]).astype(jnp.int32), axis=1)


def split_heads(matrix):
    return matrix.reshape(matrix.shape[0], HEADS, matrix.shape[1] // HEADS)


def spread_heads(per_head, model_width):
    return jnp.repeat(per_head.T, model_width // HEADS, axis=1)


def head_scores(queries, key_rows):
    score_scale = 1.0 / math.sqrt(queries.shape[1] // HEADS)
    return (
        jnp.einsum("qhd,khd->hqk", split_heads(queries), split_heads(key_rows), precision=PRECISE)
        * score_scale
    )


def mix_values(weights, value_rows):
    combined = jnp.einsum("hqk,khd->qhd", weights, split_heads(value_rows), precision=PRECISE)
    return combined.reshape(combined.shape[0], -1)


def cell_mask(query_cells, key_cells):
    return (query_cells[:, None] == key_cells[None, :])[None]


def project(layer_in, w_qkv, b_qv):
    model_width = layer_in.shape[1]
    joined = jnp.dot(layer_in, w_qkv, precision=PRECISE)
    queries = joined[:, :model_width] + b_qv[:model_width]
    key_rows = joined[:, model_width : 2 * model_width]
    value_rows = joined[:, 2 * model_width :] + b_qv[model_width:]
    return (queries, key_rows, value_rows)


def finish(
    layer_in,
    context,
    live_rows,
    w_out,
    b_out,
    gain_one,
    shift_one,
    w_in,
    b_in,
    w_back,
    b_back,
    gain_two,
    shift_two,
):
    upper_sum = layer_in + jnp.dot(context, w_out, precision=PRECISE) + b_out
    hidden = layer_norm(upper_sum, gain_one, shift_one)
    inner_act = jax.nn.gelu(jnp.dot(hidden, w_in, precision=PRECISE) + b_in, approximate=False)
    lower_sum = hidden + jnp.dot(inner_act, w_back, precision=PRECISE) + b_back
    return layer_norm(lower_sum, gain_two, shift_two) * live_rows[:, None]


def finish_local(live_rows):

    def apply_rows(given_in, given_context, *weights):
        return finish(given_in, given_context, live_rows, *weights)

    return apply_rows


def fold_keys(queries, query_cells, cell_ends, running, key_piece):
    row_max, row_total, partial_value = running
    key_rows, value_rows = key_piece
    key_cells = segments(jnp.arange(key_rows.shape[0], dtype=jnp.int32), cell_ends)
    allowed = cell_mask(query_cells, key_cells)
    masked = jnp.where(allowed, head_scores(queries, key_rows), NEGATIVE)
    new_max = jnp.maximum(row_max, jnp.max(masked, axis=2))
    weights = jnp.where(allowed, jnp.exp(masked - new_max[:, :, None]), 0.0)
    factor = jnp.exp(row_max - new_max)
    row_total = jnp.sum(weights, axis=2)
    partial_value = partial_value * spread_heads(factor, partial_value.shape[1]) + mix_values(
        weights, value_rows
    )
    return (new_max, row_total, partial_value)


def attend_back(
    queries, key_rows, value_rows, query_cells, key_cells, log_total, context, grad_context
):
    score_scale = 1.0 / math.sqrt(queries.shape[1] // HEADS)
    allowed = cell_mask(query_cells, key_cells)
    masked = jnp.where(allowed, head_scores(queries, key_rows), NEGATIVE)
    probabilities = jnp.where(allowed, jnp.exp(masked - log_total[:, :, None]), 0.0)
    grad_heads = split_heads(grad_context)
    grad_probs = jnp.einsum("qhd,khd->hqk", grad_heads, split_heads(value_rows), precision=PRECISE)
    row_dot = jnp.einsum("qhd,qhd->hq", grad_heads, split_heads(context), precision=PRECISE)
    grad_scores = probabilities * (grad_probs - row_dot[:, :, None]) * score_scale
    grad_query = jnp.einsum("hqk,khd->qhd", grad_scores, split_heads(key_rows), precision=PRECISE)
    grad_keys = jnp.einsum("hqk,qhd->khd", grad_scores, split_heads(queries), precision=PRECISE)
    grad_values = jnp.einsum("hqk,qhd->khd", probabilities, grad_heads, precision=PRECISE)
    return (
        grad_query.reshape(queries.shape),
        grad_keys.reshape(key_rows.shape),
        grad_values.reshape(key_rows.shape),
    )


def layer_forward(layer_in, params, cell_ends, positions):
    query_cells = segments(positions, cell_ends)
    live_rows = (query_cells < cell_ends.shape[0]).astype(jnp.float32)
    queries, key_rows, value_rows = project(layer_in, params[0], params[1])
    row_count = layer_in.shape[0]
    start_state = (
        jnp.full((HEADS, row_count), NEGATIVE, jnp.float32),
        jnp.zeros((HEADS, row_count), jnp.float32),
        jnp.zeros_like(layer_in),
    )
    row_max, row_total, partial_value = fold_keys(
        queries,
        query_cells,
        cell_ends,
        start_state,
        (
            lax.all_gather(key_rows, "seq", axis=0, tiled=True),
            lax.all_gather(value_rows, "seq", axis=0, tiled=True),
        ),
    )
    context = partial_value / spread_heads(row_total, layer_in.shape[1])
    log_total = row_max + jnp.log(row_total)
    kept_keys = ()
    layer_out = finish(layer_in, context, live_rows, *params[2:])
    return (layer_out, (layer_in, context, log_total, cell_ends, kept_keys))


def layer_backward(record, params, grad_out, positions):
    layer_in, context, log_total, cell_ends, kept_keys = record
    query_cells = segments(positions, cell_ends)
    live_rows = (query_cells < cell_ends.shape[0]).astype(jnp.float32)
    finish_out, finish_back = jax.vjp(finish_local(live_rows), layer_in, context, *params[2:])
    finish_grads = finish_back(grad_out)
    (queries, key_rows, value_rows), project_back = jax.vjp(project, layer_in, params[0], params[1])
    whole_keys, whole_values = (
        lax.all_gather(key_rows, "seq", axis=0, tiled=True),
        lax.all_gather(value_rows, "seq", axis=0, tiled=True),
    )
    key_cells = segments(jnp.arange(whole_keys.shape[0], dtype=jnp.int32), cell_ends)
    grad_query, grad_keys, grad_values = attend_back(
        queries,
        whole_keys,
        whole_values,
        query_cells,
        key_cells,
        log_total,
        context,
        finish_grads[1],
    )
    own_keys, own_values = (
        lax.psum_scatter(grad_keys, "seq", scatter_dimension=0, tiled=True),
        lax.psum_scatter(grad_values, "seq", scatter_dimension=0, tiled=True),
    )
    grad_in_pre, grad_qkv, grad_bias = project_back((grad_query, own_keys, own_values))
    return (finish_grads[0] + grad_in_pre, (grad_qkv, grad_bias) + tuple(finish_grads[2:]))


def select_tree(condition, first_tree, second_tree):
    return jax.tree.map(
        lambda former, latter: jnp.where(condition, former, latter), first_tree, second_tree
    )


def add_trees(first_tree, second_tree):
    return tuple((former + latter for former, latter in zip(first_tree, second_tree)))


def run_relay(activations, cotangent, cell_table, own_params, positions, is_first):
    micro_count = activations.shape[0]
    half_count = micro_count // 2
    received = jnp.zeros_like(activations[0])
    records = []
    outputs = []
    arrivals = []
    for step_index in range(micro_count + 1):
        first_batch = min(step_index, micro_count - 1)
        second_batch = max(step_index - 1, 0)
        cell_ends = jnp.where(is_first, cell_table[first_batch], cell_table[second_batch])
        layer_in = jnp.where(is_first, activations[first_batch], received)
        layer_out, record = layer_forward(layer_in, own_params, cell_ends, positions)
        records.append(record)
        outputs.append(layer_out)
        if step_index < micro_count:
            received = from_behind(layer_out, "pipe", 1)
            arrivals.append(received)
    final_output = jnp.stack(
        [
            jnp.where(is_first, arrivals[slot_index + 1], outputs[half_count + slot_index + 1])
            for slot_index in range(half_count)
        ]
    )
    grad_received = jnp.zeros_like(activations[0])
    grad_totals = tuple((jnp.zeros_like(weight) for weight in own_params))
    own_grads = []
    grad_arrivals = []
    for step_index in range(micro_count + 1):
        second_batch = min(step_index, micro_count - 1)
        first_live = 1.0 if step_index >= 1 else 0.0
        second_live = 1.0 if step_index < micro_count else 0.0
        record = select_tree(
            is_first, records[max(step_index - 1, 0)], records[min(step_index + 1, micro_count)]
        )
        upstream = jnp.where(
            is_first, grad_received * first_live, cotangent[second_batch] * second_live
        )
        grad_in, layer_grads = layer_backward(record, own_params, upstream, positions)
        grad_totals = add_trees(grad_totals, layer_grads)
        own_grads.append(grad_in)
        grad_received = from_behind(grad_in, "pipe", 1)
        grad_arrivals.append(grad_received)
    input_grad = jnp.stack(
        [
            jnp.where(
                is_first, own_grads[slot_index + 1], grad_arrivals[half_count + slot_index + 1]
            )
            for slot_index in range(half_count)
        ]
    )
    return (final_output, input_grad, tuple((total[None] for total in grad_totals)))


def reduce_grads(local_grads):
    (
        grad_w_qkv,
        grad_b_qv,
        grad_w_out,
        grad_b_out,
        grad_gain_one,
        grad_shift_one,
        grad_w_in,
        grad_b_in,
        grad_w_back,
        grad_b_back,
        grad_gain_two,
        grad_shift_two,
    ) = local_grads
    return lax.psum(
        (
            grad_w_qkv,
            grad_b_qv,
            grad_w_out,
            grad_b_out,
            grad_gain_one,
            grad_shift_one,
            grad_w_in,
            grad_b_in,
            grad_w_back,
            grad_b_back,
            grad_gain_two,
            grad_shift_two,
        ),
        ("dp", "seq"),
    )


def body(
    activations,
    cotangent,
    cell_lengths,
    w_qkv,
    b_qv,
    w_out,
    b_out,
    gain_one,
    shift_one,
    w_in,
    b_in,
    w_back,
    b_back,
    gain_two,
    shift_two,
):
    row_count = activations.shape[1]
    positions = lax.axis_index("seq") * row_count + jnp.arange(row_count, dtype=jnp.int32)
    cell_table = jnp.cumsum(cell_lengths[:, 0, :], axis=1)
    section_index = lax.axis_index("pipe")
    is_first = section_index == 0
    own_params = (
        w_qkv[0],
        b_qv[0],
        w_out[0],
        b_out[0],
        gain_one[0],
        shift_one[0],
        w_in[0],
        b_in[0],
        w_back[0],
        b_back[0],
        gain_two[0],
        shift_two[0],
    )
    final_output, input_grad, local_grads = run_relay(
        activations, cotangent, cell_table, own_params, positions, is_first
    )
    reduced = reduce_grads(local_grads)
    return (final_output, input_grad) + tuple(reduced)


def solution(mesh):
    in_specs = (
        P(None, ("dp", "seq"), None),
        P(None, ("dp", "seq"), None),
        P(None, "dp", None),
        P("pipe", None, None),
        P("pipe", None),
        P("pipe", None, None),
        P("pipe", None),
        P("pipe", None),
        P("pipe", None),
        P("pipe", None, None),
        P("pipe", None),
        P("pipe", None, None),
        P("pipe", None),
        P("pipe", None),
        P("pipe", None),
    )
    out_specs = (
        P("pipe", ("dp", "seq"), None),
        P("pipe", ("dp", "seq"), None),
        P("pipe", None, None),
        P("pipe", None),
        P("pipe", None, None),
        P("pipe", None),
        P("pipe", None),
        P("pipe", None),
        P("pipe", None, None),
        P("pipe", None),
        P("pipe", None, None),
        P("pipe", None),
        P("pipe", None),
        P("pipe", None),
    )
    return jax.shard_map(body, mesh=mesh, in_specs=in_specs, out_specs=out_specs, check_vma=False)
```

profile of v0, /device:TPU:0, one launch (start us, length us, event | category | flops | bytes accessed | tf_op | source)
XLA Modules:
  0.0 1353.2 jit_solution(13635230348770425676)
XLA Ops:
  16.0 24.0 %all-gather.21.cloned.1.call-done = f32[1024,256]{1,0:T(8,128)} async-done(((f32[512,256]{1,0:T(8,128)}), f32[1024,256]{1,0:T(8,128)}) %all-gather.21.cloned.1.call-update) | async-done | bytes 1048592 | tf_op jit(solution)/shard_map/all_gather | solution.py:149
  69.7 11.8 fusion.435
  100.1 21.1 %all-gather.25.cloned.1.call-done = f32[1024,256]{1,0:T(8,128)} async-done(((f32[512,256]{1,0:T(8,128)}), f32[1024,256]{1,0:T(8,128)}) %all-gather.25.cloned.1.call-update) | async-done | bytes 1048592 | tf_op jit(solution)/shard_map/all_gather | solution.py:149
  123.7 9.6 fusion.1
  150.6 11.8 fusion.434
  181.4 21.8 %all-gather.29.cloned.1.call-done = f32[1024,256]{1,0:T(8,128)} async-done(((f32[512,256]{1,0:T(8,128)}), f32[1024,256]{1,0:T(8,128)}) %all-gather.29.cloned.1.call-update) | async-done | bytes 1048592 | tf_op jit(solution)/shard_map/all_gather | solution.py:149
  205.7 9.4 fusion.2
  232.6 11.8 fusion.433
  264.0 21.1 %all-gather.33.cloned.1.call-done = f32[1024,256]{1,0:T(8,128)} async-done(((f32[512,256]{1,0:T(8,128)}), f32[1024,256]{1,0:T(8,128)}) %all-gather.33.cloned.1.call-update) | async-done | bytes 1048592 | tf_op jit(solution)/shard_map/all_gather | solution.py:149
  287.7 9.6 fusion.3
  314.7 11.8 fusion.432
  362.3 10.0 fusion.1040
  374.6 12.1 all-gather.37.cloned.1.call-done
  389.2 9.6 fusion.4
  415.7 14.0 %broadcast_select_fusion.1 = (f32[512,4,64]{0,2,1:T(8,128)}, f32[512,4,64]{0,2,1:T(8,128)}, f32[512,4,64]{0,2,1:T(8,128)}, f32[512,4,64]{0,2,1:T(8,128)S(1)}, f32[512,4,64]{0,2,1:T(8,128)}, /*index=5*/f32[512,4,64]{0,2,1:T(8,128)}) fusion(f32[512,4,64]{0,2,1:T(8,128)} %copy-done.113, pred[]{:T(512)S(6)} %eq.173, f32[512,4,64]{0,2,1:T(8,128)} %copy-done.114, ...), kind=kOutput, calls=%fused_computation.1063 | convolution fusion | flops 1619918848 | bytes 15228929 | tf_op jit(solution)/shard_map/hqk,khd->qhd/dot_general | solution.py:49
  453.1 12.6 multiply_multiply_fusion.4
  482.6 10.0 fusion.1042
  493.1 12.6 bitcast_reduce_fusion.4
  547.0 12.5 multiply_multiply_fusion.3
  575.3 10.0 fusion.1044
  603.3 20.4 %reduce-scatter.17.cloned.1.call-done = f32[512,256]{0,1:T(8,128)} async-done(((f32[1024,256]{0,1:T(8,128)}), f32[512,256]{0,1:T(8,128)}) %reduce-scatter.17.cloned.1.call-update) | async-done | bytes 524304 | tf_op jit(solution)/shard_map/reduce_scatter | solution.py:183
  652.5 12.6 multiply_multiply_fusion.2
  713.4 10.3 fusion.1046
  723.7 11.4 bitcast_reduce_fusion.2
  740.6 14.7 %all-gather.57.cloned.1.call-done = f32[1024,256]{1,0:T(8,128)} async-done(((f32[512,256]{1,0:T(8,128)}), f32[1024,256]{1,0:T(8,128)}) %all-gather.57.cloned.1.call-update) | async-done | bytes 1048592 | tf_op jit(solution)/shard_map/all_gather | solution.py:168
  757.9 10.5 fusion.1048
  790.7 17.4 %all-gather.59.cloned.1.call-done = f32[1024,256]{1,0:T(8,128)} async-done(((f32[512,256]{1,0:T(8,128)}), f32[1024,256]{1,0:T(8,128)}) %all-gather.59.cloned.1.call-update) | async-done | bytes 1048592 | tf_op jit(solution)/shard_map/all_gather | solution.py:169
  820.4 12.6 multiply_multiply_fusion.1
  867.2 11.3 bitcast_reduce_fusion.1
  919.5 12.7 multiply_multiply_fusion
  947.3 12.6 bitcast_reduce_fusion
  986.3 348.8 %all-reduce.25 = (f32[1,512]{1,0:T(1,128)}, f32[1,256]{1,0:T(1,128)}, f32[1,256]{1,0:T(1,128)}, f32[1,256]{1,0:T(1,128)}, f32[1,512]{1,0:T(1,128)}, /*index=5*/f...) all-reduce(f32[1,512]{1,0:T(1,128)S(1)} %bitcast.790, ...), channel_id=1, replica_groups=mesh['pipe'=2,'dp'=32,'seq'=2] {'dp','seq'}, use_global_device_ids=true, to_apply=%region_112.113 | all-reduce | flops 2560 | bytes 20480 | tf_op jit(solution)/shard_map/psum | solution.py:269
  (789 shorter events, 572.7 us)
Async XLA Ops:
  7.2 32.8 %all-gather.21.cloned.1.call-start = ((), (), s32[]{:S(2)}) async-start(), calls=%async_computation.10 | async-start | bytes 1572864 | tf_op jit(solution)/shard_map/all_gather | solution.py:149
  13.5 53.5 %all-gather.23.cloned.1.call-start = ((), (), s32[]{:S(2)}) async-start(), calls=%async_computation.11 | async-start | bytes 1572864 | tf_op jit(solution)/shard_map/all_gather | solution.py:150
  14.3 106.9 %all-gather.25.cloned.1.call-start = ((), (), s32[]{:S(2)}) async-start(), calls=%async_computation.12 | async-start | bytes 1572864 | tf_op jit(solution)/shard_map/all_gather | solution.py:149
  96.3 51.8 %all-gather.27.cloned.1.call-start = ((), (), s32[]{:S(2)}) async-start(), calls=%async_computation.13 | async-start | bytes 1572864 | tf_op jit(solution)/shard_map/all_gather | solution.py:150
  99.7 103.5 %all-gather.29.cloned.1.call-start = ((), (), s32[]{:S(2)}) async-start(), calls=%async_computation.14 | async-start | bytes 1572864 | tf_op jit(solution)/shard_map/all_gather | solution.py:149
  178.1 52.0 %all-gather.31.cloned.1.call-start = ((), (), s32[]{:S(2)}) async-start(), calls=%async_computation.15 | async-start | bytes 1572864 | tf_op jit(solution)/shard_map/all_gather | solution.py:150
  180.9 104.2 %all-gather.33.cloned.1.call-start = ((), (), s32[]{:S(2)}) async-start(), calls=%async_computation.16 | async-start | bytes 1572864 | tf_op jit(solution)/shard_map/all_gather | solution.py:149
  260.2 52.0 %all-gather.35.cloned.1.call-start = ((), (), s32[]{:S(2)}) async-start(), calls=%async_computation.17 | async-start | bytes 1572864 | tf_op jit(solution)/shard_map/all_gather | solution.py:150
  263.6 96.2 %all-gather.41.cloned.1.call-start = ((), (), s32[]{:S(2)}) async-start(), calls=%async_computation.20 | async-start | bytes 1572864 | tf_op jit(solution)/shard_map/all_gather | solution.py:168
  334.7 52.0 %all-gather.37.cloned.1.call-start = ((), (), s32[]{:S(2)}) async-start(), calls=%async_computation.18 | async-start | bytes 1572864 | tf_op jit(solution)/shard_map/all_gather | solution.py:149
  346.7 66.5 %all-gather.39.cloned.1.call-start = ((), (), s32[]{:S(2)}) async-start(), calls=%async_computation.19 | async-start | bytes 1572864 | tf_op jit(solution)/shard_map/all_gather | solution.py:150
  347.4 103.1 %all-gather.43.cloned.1.call-start = ((), (), s32[]{:S(2)}) async-start(), calls=%async_computation.22 | async-start | bytes 1572864 | tf_op jit(solution)/shard_map/all_gather | solution.py:169
  351.3 128.6 %all-gather.45.cloned.1.call-start = ((), (), s32[]{:S(2)}) async-start(), calls=%async_computation.24 | async-start | bytes 1572864 | tf_op jit(solution)/shard_map/all_gather | solution.py:168
  372.3 141.8 %reduce-scatter.11.cloned.1.call-start = ((), (), s32[]{:S(2)}) async-start(), calls=%async_computation.21 | async-start | bytes 1572864 | tf_op jit(solution)/shard_map/reduce_scatter | solution.py:184
  450.5 67.7 %reduce-scatter.13.cloned.1.call-start = ((), (), s32[]{:S(2)}) async-start(), calls=%async_computation.23 | async-start | bytes 1572864 | tf_op jit(solution)/shard_map/reduce_scatter | solution.py:183
  475.2 69.3 %all-gather.47.cloned.1.call-start = ((), (), s32[]{:S(2)}) async-start(), calls=%async_computation.26 | async-start | bytes 1572864 | tf_op jit(solution)/shard_map/all_gather | solution.py:169
  477.3 95.3 %all-gather.49.cloned.1.call-start = ((), (), s32[]{:S(2)}) async-start(), calls=%async_computation.28 | async-start | bytes 1572864 | tf_op jit(solution)/shard_map/all_gather | solution.py:168
  492.6 110.7 %reduce-scatter.15.cloned.1.call-start = ((), (), s32[]{:S(2)}) async-start(), calls=%async_computation.25 | async-start | bytes 1572864 | tf_op jit(solution)/shard_map/reduce_scatter | solution.py:184
  543.3 80.4 %reduce-scatter.17.cloned.1.call-start = ((), (), s32[]{:S(2)}) async-start(), calls=%async_computation.27 | async-start | bytes 1572864 | tf_op jit(solution)/shard_map/reduce_scatter | solution.py:183
  568.9 81.1 %all-gather.51.cloned.1.call-start = ((), (), s32[]{:S(2)}) async-start(), calls=%async_computation.30 | async-start | bytes 1572864 | tf_op jit(solution)/shard_map/all_gather | solution.py:169
  570.0 140.9 %all-gather.53.cloned.1.call-start = ((), (), s32[]{:S(2)}) async-start(), calls=%async_computation.32 | async-start | bytes 1572864 | tf_op jit(solution)/shard_map/all_gather | solution.py:168
  585.3 149.7 %reduce-scatter.19.cloned.1.call-start = ((), (), s32[]{:S(2)}) async-start(), calls=%async_computation.29 | async-start | bytes 1572864 | tf_op jit(solution)/shard_map/reduce_scatter | solution.py:184
  649.1 86.0 %reduce-scatter.21.cloned.1.call-start = ((), (), s32[]{:S(2)}) async-start(), calls=%async_computation.31 | async-start | bytes 1572864 | tf_op jit(solution)/shard_map/reduce_scatter | solution.py:183
  674.6 80.7 %all-gather.57.cloned.1.call-start = ((), (), s32[]{:S(2)}) async-start(), calls=%async_computation.36 | async-start | bytes 1572864 | tf_op jit(solution)/shard_map/all_gather | solution.py:168
  675.1 113.0 %all-gather.55.cloned.1.call-start = ((), (), s32[]{:S(2)}) async-start(), calls=%async_computation.34 | async-start | bytes 1572864 | tf_op jit(solution)/shard_map/all_gather | solution.py:169
  675.9 132.2 %all-gather.59.cloned.1.call-start = ((), (), s32[]{:S(2)}) async-start(), calls=%async_computation.38 | async-start | bytes 1572864 | tf_op jit(solution)/shard_map/all_gather | solution.py:169
  684.7 193.9 %reduce-scatter.23.cloned.1.call-start = ((), (), s32[]{:S(2)}) async-start(), calls=%async_computation.33 | async-start | bytes 1572864 | tf_op jit(solution)/shard_map/reduce_scatter | solution.py:184
  785.6 93.0 %reduce-scatter.25.cloned.1.call-start = ((), (), s32[]{:S(2)}) async-start(), calls=%async_computation.35 | async-start | bytes 1572864 | tf_op jit(solution)/shard_map/reduce_scatter | solution.py:183
  842.3 132.8 %reduce-scatter.27.cloned.1.call-start = ((), (), s32[]{:S(2)}) async-start(), calls=%async_computation.37 | async-start | bytes 1572864 | tf_op jit(solution)/shard_map/reduce_scatter | solution.py:184
  910.0 65.2 %reduce-scatter.29.cloned.1.call-start = ((), (), s32[]{:S(2)}) async-start(), calls=%async_computation.39 | async-start | bytes 1572864 | tf_op jit(solution)/shard_map/reduce_scatter | solution.py:183
  941.6 397.1 %all-reduce.29.cloned.1.call-start = ((), (), s32[]{:S(2)}) async-start(), calls=%async_computation.40 | async-start | bytes 4194304 | tf_op jit(solution)/shard_map/psum | solution.py:269
  985.9 349.2 %collective-permute-start.8 = (f32[512,256]{0,1:T(8,128)S(1)}, f32[512,256]{0,1:T(8,128)S(1)}, u32[]{:S(2)}, u32[]{:S(2)}) collective-permute-start(f32[512,256]{0,1:T(8,128)S(1)} %convolution_add_fusion.34), channel_id=1, source_target_pairs={{64,0},{0,64},{65,1},{1,65},{66,2},{2,66},{67,3},{3,67},{68,4},{4,... | collective-permute-start | bytes 1572872 | tf_op jit(solution)/shard_map/ppermute | solution.py:19
  (186 other events, 2275.7 us)
Sparse Core Ops, SparseCore 0:
  13.6 26.3 all-gather.20
  42.2 24.7 all-gather.22
  96.4 24.7 all-gather.24
  123.3 24.7 all-gather.26
  178.2 24.8 all-gather.28
  205.2 24.7 all-gather.30
  260.3 24.7 all-gather.32
  287.4 24.7 all-gather.34
  334.8 24.9 all-gather.40
  361.9 24.7 all-gather.36
  388.4 24.7 all-gather.38
  414.7 24.7 all-gather.42
  441.2 24.7 all-gather.44
  468.2 23.7 reduce-scatter.10
  494.3 23.7 reduce-scatter.12
  519.7 24.7 all-gather.46
  546.0 24.7 all-gather.48
  573.0 23.7 reduce-scatter.14
  599.9 23.7 reduce-scatter.16
  625.2 24.7 all-gather.50
  651.7 24.7 all-gather.52
  678.9 23.7 reduce-scatter.18
  705.2 23.7 reduce-scatter.20
  730.5 24.7 all-gather.56
  757.0 24.7 all-gather.54
  783.3 24.7 all-gather.58
  810.3 23.7 reduce-scatter.22
  842.4 23.8 reduce-scatter.24
  910.1 23.8 reduce-scatter.26
  941.7 23.9 reduce-scatter.28
  983.2 134.5 all-reduce.28
where the time goes:
time: 1360 us; the launch traced here: 1350 us
  matrix products  541 us (40%)
  blocking collectives  349 us (26%)
  waiting for transfers between devices  212 us (16%)
  local copies, waits for them, and re-layouts  140 us (10%)
  other arithmetic  86.2 us (6%)
  between operations  18 us (1%)
    psum x1, blocking collectives, reduce_grads(): lax.psum((grad_w_qkv, grad_b_qv, grad_w_out, grad_b_out, grad_gain_one, g...  349 us
    all_gather x5, waiting for transfers between devices, layer_forward(): lax.all_gather(key_rows, 'seq', axis=0, tiled=True)  100 us
    dot_general x10, matrix products, head_scores(): jnp.einsum('qhd,khd->hqk', split_heads(queries), split_heads(key_rows), p...  98.4 us
    dot_general x20, matrix products, finish(): lower_sum = hidden + jnp.dot(inner_act, w_back, precision=PRECISE) + b_back  65.9 us
    unnamed x371, local copies, waits for them, and re-layouts  64.3 us
    dot_general x5, matrix products, attend_back(): jnp.einsum('qhd,khd->hqk', grad_heads, split_heads(value_rows), precision...  62.9 us
    dot_general x5, matrix products, mix_values(): jnp.einsum('hqk,khd->qhd', weights, split_heads(value_rows), precision=PR...  61.1 us
    dot_general x5, matrix products, attend_back(): jnp.einsum('hqk,khd->qhd', grad_scores, split_heads(key_rows), precision=...  56.9 us
  transfers between devices with their start and end apart: 40, of which 23 were waited for; matrix products, arithmetic and copies ran while one was open for 43% of the time, Pallas kernels for 0%

commit v1 on v0

v1 whole, which is shorter than its diff:
```python
import math

import jax
import jax.numpy as jnp
from jax import lax
from jax.experimental import pallas as pl
from jax.experimental.pallas import tpu as pltpu
from jax.sharding import PartitionSpec as P

MESH = pl.DeviceIdType.MESH
F32 = jnp.float32
BF16 = jnp.bfloat16

HEADS = 4
HEAD = 64
WIDTH = 256
INNER = 512
HALF = 512
SLOT = 1024
BLOCK = 256
BLOCKS = SLOT // BLOCK
EPSILON = 1e-06
APART = -1e30
LOG2E = math.log2(math.e)
LN2 = math.log(2.0)
QUERY_SCALE = LOG2E / math.sqrt(HEAD)
KEY_SCALE = 1.0 / math.sqrt(HEAD)

AT_QKV, AT_OUT, AT_IN, AT_BACK, AT_SMALL = 0, 768, 1024, 1536, 2048
MATRIX_ROWS = 2048
SMALL_ROWS = 16
PACKED_ROWS = MATRIX_ROWS + SMALL_ROWS
V_Q, V_V, V_OUT, V_GAIN1, V_SHIFT1, V_IN, V_BACK, V_GAIN2, V_SHIFT2 = 0, 1, 2, 3, 4, 5, 7, 8, 9


def dot(left, right, left_t=False, right_t=False):
    dims = (((0 if left_t else 1,), (1 if right_t else 0,)), ((), ()))
    return lax.dot_general(left, right, dims, preferred_element_type=F32)


def split(values):
    high = values.astype(BF16)
    return high, (values - high.astype(F32)).astype(BF16)


def dot3(left_high, left_low, right_high, right_low, right_t=False):
    return (
        dot(left_high, right_high, right_t=right_t)
        + dot(left_high, right_low, right_t=right_t)
        + dot(left_low, right_high, right_t=right_t)
    )


def col_mean(values):
    return jnp.mean(values, axis=0, keepdims=True)


def norm_rows(values):
    center = values - col_mean(values)
    spread = col_mean(center * center)
    inverse = lax.rsqrt(spread + EPSILON)
    return center * inverse, inverse


def norm_back(grad, normed, inverse):
    return (grad - col_mean(grad) - normed * col_mean(grad * normed)) * inverse


def feature_tile(base, values, first):
    high = values.astype(BF16).astype(F32)
    rest = values - high
    middle = rest.astype(BF16).astype(F32)
    low = rest - middle
    row = lax.broadcasted_iota(jnp.int32, base.shape, 0)
    tile = jnp.where(row == first, high, base)
    tile = jnp.where(row == first + 1, middle, tile)
    return jnp.where(row == first + 2, low, tile).astype(BF16)


def lane_fold(values):
    folded = values[:, :128]
    for first in range(128, values.shape[1], 128):
        folded = folded + values[:, first:first + 128]
    return folded


def relay_kernel(
    act_ref, cot_ref, len_ref, w_qkv_ref, w_out_ref, w_in_ref, w_back_ref, vec_ref,
    final_ref, grad_ref, packed_ref,
    x_in, c_in, w_qkv, w_out, w_in, w_back, vecs,
    fq, fo, fi, fb, nq, no, ni, nb, cols,
    marks, live, x_now, x_parts, q_all, k_all, v_all, ctx_parts,
    n_one, r_one, hid_parts, slope, inner_parts, n_two, r_two,
    d_now, dl_parts, dp_parts, du_now, du_parts, do_all, dkv, dqkv, sums, packed,
    local_sem, send_sem, recv_sem,
):
    core = lax.axis_index("pipe")
    half = lax.axis_index("seq")
    sibling = {"pipe": 1 - core}
    partner = {"seq": 1 - half}

    barrier = pltpu.get_barrier_semaphore()
    pl.semaphore_signal(barrier, inc=1, device_id=sibling, device_id_type=MESH)
    pl.semaphore_signal(barrier, inc=1, device_id=partner, device_id_type=MESH)
    pl.semaphore_wait(barrier, 2)

    def remote(src, dst, index, device):
        return pltpu.make_async_remote_copy(
            src_ref=src, dst_ref=dst, send_sem=send_sem.at[index], recv_sem=recv_sem.at[index],
            device_id=device, device_id_type=MESH,
        )

    mine = 2 * core + half
    theirs = 2 * core + 1 - half
    weight_pairs = (
        (w_qkv_ref, w_qkv), (w_out_ref, w_out), (w_in_ref, w_in), (w_back_ref, w_back), (vec_ref, vecs),
    )
    x_send = remote(act_ref.at[theirs], x_in.at[1], 0, partner)
    c_send = remote(cot_ref.at[theirs], c_in.at[1], 1, partner)
    w_sends = [remote(src.at[0], dst.at[core], 2 + i, sibling) for i, (src, dst) in enumerate(weight_pairs)]
    x_own = pltpu.make_async_copy(act_ref.at[mine], x_in.at[0], local_sem.at[0])
    c_own = pltpu.make_async_copy(cot_ref.at[mine], c_in.at[0], local_sem.at[1])
    w_owns = [
        pltpu.make_async_copy(src.at[0], dst.at[core], local_sem.at[2 + i])
        for i, (src, dst) in enumerate(weight_pairs)
    ]
    x_send.start()
    for copy in w_sends:
        copy.start()
    x_own.start()
    for copy in w_owns:
        copy.start()
    c_own.start()

    lane = lax.broadcasted_iota(jnp.int32, (16, SLOT), 1)
    row = lax.broadcasted_iota(jnp.int32, (16, SLOT), 0)
    place = jnp.where(lane < HALF, half * HALF + lane, (1 - half) * HALF + lane - HALF)
    end_0 = len_ref[mine, 0, 0]
    end_1 = end_0 + len_ref[mine, 0, 1]
    end_2 = end_1 + len_ref[mine, 0, 2]
    one = jnp.ones_like(place)
    none = jnp.zeros_like(place)
    cell = (
        jnp.where(place >= end_0, one, none)
        + jnp.where(place >= end_1, one, none)
        + jnp.where(place >= end_2, one, none)
    )
    same = jnp.where(cell == row, 1.0, 0.0)
    marks[...] = same
    live[...] = jnp.where(cell < 3, 1.0, 0.0)[:8]
    key_marks = jnp.where(row < 4, (1.0 - same) * APART, jnp.where(row < 7, 1.0, 0.0)).astype(BF16)
    value_marks = jnp.where(row < 3, 1.0, 0.0).astype(BF16)
    query_marks = same.astype(BF16)
    blank = jnp.zeros((48, SLOT), BF16)
    for layer in range(2):
        for head in range(HEADS):
            q_all[layer, head, 192:208, :] = query_marks
            k_all[layer, head, 192:208, :] = key_marks
            v_all[layer, head, 192:208, :] = value_marks
            q_all[layer, head, 208:256, :] = blank
            k_all[layer, head, 208:256, :] = blank
            v_all[layer, head, 208:256, :] = blank
    for head in range(HEADS):
        do_all[head, 208:256, :] = blank

    for copy in w_owns:
        copy.wait()
    for copy in w_sends:
        copy.wait()
    x_own.wait()
    x_send.wait()
    c_send.start()

    first_x = jnp.concatenate([x_in[0].T, x_in[1].T], axis=1)
    x_now[...] = first_x

    def forward(layer, carry):
        cols[...] = jnp.concatenate([vecs[layer].T, jnp.zeros((WIDTH, 128 - SMALL_ROWS), F32)], axis=1)

        def col(index):
            return cols[:, index:index + 1]

        fq[0], fq[1] = split(w_qkv[layer].T)
        fo[0], fo[1] = split(w_out[layer].T)
        fi[0], fi[1] = split(w_in[layer].T)
        fb[0], fb[1] = split(w_back[layer].T)
        x_parts[layer, 0], x_parts[layer, 1] = split(x_now[...])

        for block in range(BLOCKS):
            at = slice(block * BLOCK, (block + 1) * BLOCK)
            joined = dot3(fq[0], fq[1], x_parts[layer, 0, :, at], x_parts[layer, 1, :, at])
            q_high, q_low = split((joined[:WIDTH] + col(V_Q)) * QUERY_SCALE)
            k_high, k_low = split(joined[WIDTH:2 * WIDTH])
            v_high, v_low = split(joined[2 * WIDTH:] + col(V_V))
            for head in range(HEADS):
                rows = slice(head * HEAD, (head + 1) * HEAD)
                q_all[layer, head, 0:64, at] = q_high[rows]
                q_all[layer, head, 64:128, at] = q_high[rows]
                q_all[layer, head, 128:192, at] = q_low[rows]
                k_all[layer, head, 0:64, at] = k_high[rows]
                k_all[layer, head, 64:128, at] = k_low[rows]
                k_all[layer, head, 128:192, at] = k_high[rows]
                v_all[layer, head, 0:64, at] = v_high[rows]
                v_all[layer, head, 64:128, at] = v_low[rows]
                v_all[layer, head, 128:192, at] = v_high[rows]

        def attend(head, inside):
            rows = pl.ds(pl.multiple_of(head * HEAD, HEAD), HEAD)
            for block in range(BLOCKS):
                at = slice(block * BLOCK, (block + 1) * BLOCK)
                scores = dot(k_all[layer, head], q_all[layer, head, :, at], left_t=True)
                top = jnp.max(scores, axis=0, keepdims=True)
                weights = jnp.exp2(scores - top)
                total = jnp.sum(weights, axis=0, keepdims=True)
                high, low = split(weights)
                both = dot(v_all[layer, head, 0:128, :], high)
                context = both[:64] + both[64:] + dot(v_all[layer, head, 0:64, :], low)
                context = context / total
                ctx_parts[layer, 0, rows, at], ctx_parts[layer, 1, rows, at] = split(context)
                log_total = top + jnp.log(total) * LOG2E
                q_all[layer, head, 192:208, at] = feature_tile(marks[:, at], -log_total, 4)
            return inside

        lax.fori_loop(0, HEADS, attend, 0)

        for block in range(BLOCKS):
            at = slice(block * BLOCK, (block + 1) * BLOCK)
            upper = x_now[:, at] + dot3(fo[0], fo[1], ctx_parts[layer, 0, :, at], ctx_parts[layer, 1, :, at]) + col(V_OUT)
            normed, inverse = norm_rows(upper)
            n_one[layer, :, at] = normed
            r_one[layer, :, at] = inverse
            hidden = normed * col(V_GAIN1) + col(V_SHIFT1)
            hid_high, hid_low = split(hidden)
            hid_parts[layer, 0, :, at] = hid_high
            hid_parts[layer, 1, :, at] = hid_low
            in_bias = jnp.concatenate([col(V_IN), col(V_IN + 1)], axis=0)
            pre = dot3(fi[0], fi[1], hid_high, hid_low) + in_bias
            share = 0.5 + 0.5 * lax.erf(pre * math.sqrt(0.5))
            slope[layer, :, at] = share + pre * (jnp.exp(pre * pre * -0.5) * (1.0 / math.sqrt(2.0 * math.pi)))
            inner_high, inner_low = split(pre * share)
            inner_parts[layer, 0, :, at] = inner_high
            inner_parts[layer, 1, :, at] = inner_low
            lower = hidden + dot3(fb[0], fb[1], inner_high, inner_low) + col(V_BACK)
            normed, inverse = norm_rows(lower)
            n_two[layer, :, at] = normed
            r_two[layer, :, at] = inverse
            x_now[:, at] = live[0:1, at] * (normed * col(V_GAIN2) + col(V_SHIFT2))
        return carry

    lax.fori_loop(0, 2, forward, 0)

    x_in[0] = x_now[:, :HALF].T
    x_in[1] = x_now[:, HALF:].T
    y_send = remote(x_in.at[1], final_ref.at[half], 7, partner)
    y_own = pltpu.make_async_copy(x_in.at[0], final_ref.at[half], local_sem.at[7])
    y_send.start()
    y_own.start()

    c_own.wait()
    c_send.wait()
    first_d = jnp.concatenate([c_in[0].T, c_in[1].T], axis=1)
    d_now[...] = first_d

    def backward(step, carry):
        layer = 1 - step
        cols[...] = jnp.concatenate([vecs[layer].T, jnp.zeros((WIDTH, 128 - SMALL_ROWS), F32)], axis=1)

        def col(index):
            return cols[:, index:index + 1]

        nq[0], nq[1] = split(w_qkv[layer])
        no[0], no[1] = split(w_out[layer])
        ni[0], ni[1] = split(w_in[layer])
        nb[0], nb[1] = split(w_back[layer])
        sums[...] = jnp.zeros_like(sums)

        def add_sum(index, values):
            sums[index] += lane_fold(values)

        for block in range(BLOCKS):
            at = slice(block * BLOCK, (block + 1) * BLOCK)
            grad = live[0:1, at] * d_now[:, at]
            normed = n_two[layer, :, at]
            add_sum(V_GAIN2, grad * normed)
            add_sum(V_SHIFT2, grad)
            d_lower = norm_back(grad * col(V_GAIN2), normed, r_two[layer, :, at])
            add_sum(V_BACK, d_lower)
            high, low = split(d_lower)
            dl_parts[0, :, at] = high
            dl_parts[1, :, at] = low
            d_pre = dot3(nb[0], nb[1], high, low) * slope[layer, :, at]
            add_sum(V_IN, d_pre[:WIDTH])
            add_sum(V_IN + 1, d_pre[WIDTH:])
            high, low = split(d_pre)
            dp_parts[0, :, at] = high
            dp_parts[1, :, at] = low
            d_hidden = d_lower + dot3(ni[0], ni[1], high, low)
            normed = n_one[layer, :, at]
            add_sum(V_GAIN1, d_hidden * normed)
            add_sum(V_SHIFT1, d_hidden)
            d_upper = norm_back(d_hidden * col(V_GAIN1), normed, r_one[layer, :, at])
            add_sum(V_OUT, d_upper)
            du_now[:, at] = d_upper
            high, low = split(d_upper)
            du_parts[0, :, at] = high
            du_parts[1, :, at] = low
            d_context = dot3(no[0], no[1], high, low)
            high, low = split(d_context)
            context = ctx_parts[layer, 0, :, at].astype(F32) + ctx_parts[layer, 1, :, at].astype(F32)
            product = d_context * context
            for head in range(HEADS):
                rows = slice(head * HEAD, (head + 1) * HEAD)
                do_all[head, 0:64, at] = high[rows]
                do_all[head, 64:128, at] = high[rows]
                do_all[head, 128:192, at] = low[rows]
                row_dot = jnp.sum(product[rows], axis=0, keepdims=True)
                do_all[head, 192:208, at] = feature_tile(jnp.zeros((16, BLOCK), F32), -row_dot, 0)

        packed[layer, AT_BACK:AT_BACK + INNER, :] = dot3(
            inner_parts[layer, 0], inner_parts[layer, 1], dl_parts[0], dl_parts[1], right_t=True)
        for part in range(2):
            rows = slice(part * WIDTH, (part + 1) * WIDTH)
            packed[layer, AT_IN + part * WIDTH:AT_IN + (part + 1) * WIDTH, :] = dot3(
                hid_parts[layer, 0], hid_parts[layer, 1], dp_parts[0, rows], dp_parts[1, rows], right_t=True)
        packed[layer, AT_OUT:AT_OUT + WIDTH, :] = dot3(
            ctx_parts[layer, 0], ctx_parts[layer, 1], du_parts[0], du_parts[1], right_t=True)

        def attend_back(head, inside):
            rows = pl.ds(pl.multiple_of(head * HEAD, HEAD), HEAD)
            for block in range(2):
                at = slice(block * HALF, (block + 1) * HALF)
                probs = jnp.exp2(dot(q_all[layer, head, :, at], k_all[layer, head], left_t=True))
                d_scores = probs * dot(do_all[head, :, at], v_all[layer, head], left_t=True)
                p_high, p_low = split(probs)
                s_high, s_low = split(d_scores)
                both = dot(k_all[layer, head, 0:128, :], s_high, right_t=True)
                d_query = (both[:64] + both[64:] + dot(k_all[layer, head, 0:64, :], s_low, right_t=True)) * KEY_SCALE
                sums[V_Q, rows, :] += lane_fold(d_query)
                dqkv[0, rows, at], dqkv[1, rows, at] = split(d_query)
                both = dot(q_all[layer, head, 64:192, at], s_high)
                d_key = both[:64] + both[64:] + dot(q_all[layer, head, 64:128, at], s_low)
                both = dot(do_all[head, 64:192, at], p_high)
                d_value = both[:64] + both[64:] + dot(do_all[head, 64:128, at], p_low)
                if block == 0:
                    dkv[0:64, :] = d_key
                    dkv[64:128, :] = d_value
                else:
                    d_key = (dkv[0:64, :] + d_key) * LN2
                    d_value = dkv[64:128, :] + d_value
                    k_rows = pl.ds(pl.multiple_of(WIDTH + head * HEAD, HEAD), HEAD)
                    v_rows = pl.ds(pl.multiple_of(2 * WIDTH + head * HEAD, HEAD), HEAD)
                    dqkv[0, k_rows, :], dqkv[1, k_rows, :] = split(d_key)
                    dqkv[0, v_rows, :], dqkv[1, v_rows, :] = split(d_value)
                    sums[V_V, rows, :] += lane_fold(d_value)
            return inside

        lax.fori_loop(0, HEADS, attend_back, 0)

        for block in range(BLOCKS):
            at = slice(block * BLOCK, (block + 1) * BLOCK)
            d_now[:, at] = du_now[:, at] + dot3(nq[0], nq[1], dqkv[0, :, at], dqkv[1, :, at])
        for part in range(3):
            rows = slice(part * WIDTH, (part + 1) * WIDTH)
            packed[layer, part * WIDTH:(part + 1) * WIDTH, :] = dot3(
                x_parts[layer, 0], x_parts[layer, 1], dqkv[0, rows], dqkv[1, rows], right_t=True)
        lane_small = lax.broadcasted_iota(jnp.int32, (WIDTH, 128), 1)
        small = jnp.zeros((WIDTH, 128), F32)
        for index in range(10):
            total = jnp.sum(sums[index], axis=1, keepdims=True)
            small = jnp.where(lane_small == index, total, small)
        packed[layer, AT_SMALL:AT_SMALL + SMALL_ROWS, :] = small.T[:SMALL_ROWS]
        return carry

    lax.fori_loop(0, 2, backward, 0)

    c_in[0] = d_now[:, :HALF].T
    c_in[1] = d_now[:, HALF:].T
    d_send = remote(c_in.at[1], grad_ref.at[half], 8, partner)
    d_own = pltpu.make_async_copy(c_in.at[0], grad_ref.at[half], local_sem.at[8])
    p_own = pltpu.make_async_copy(packed, packed_ref, local_sem.at[9])
    d_send.start()
    d_own.start()
    p_own.start()
    y_own.wait()
    y_send.wait()
    d_own.wait()
    p_own.wait()
    d_send.wait()


def relay(activations, cotangent, cell_lengths, w_qkv, w_out, w_in, w_back, vectors):
    anywhere = pl.BlockSpec(memory_space=pl.ANY)
    shape = jax.ShapeDtypeStruct
    parts = lambda rows: pltpu.VMEM((2, 2, rows, SLOT), BF16)
    return pl.pallas_call(
        relay_kernel,
        out_shape=(
            shape((2, HALF, WIDTH), F32),
            shape((2, HALF, WIDTH), F32),
            shape((2, PACKED_ROWS, WIDTH), F32),
        ),
        in_specs=[anywhere, anywhere, pl.BlockSpec(memory_space=pltpu.SMEM)] + [anywhere] * 5,
        out_specs=(anywhere, anywhere, anywhere),
        scratch_shapes=[
            pltpu.VMEM((2, HALF, WIDTH), F32),
            pltpu.VMEM((2, HALF, WIDTH), F32),
            pltpu.VMEM((2, WIDTH, 3 * WIDTH), F32),
            pltpu.VMEM((2, WIDTH, WIDTH), F32),
            pltpu.VMEM((2, WIDTH, INNER), F32),
            pltpu.VMEM((2, INNER, WIDTH), F32),
            pltpu.VMEM((2, SMALL_ROWS, WIDTH), F32),
            pltpu.VMEM((2, 3 * WIDTH, WIDTH), BF16),
            pltpu.VMEM((2, WIDTH, WIDTH), BF16),
            pltpu.VMEM((2, INNER, WIDTH), BF16),
            pltpu.VMEM((2, WIDTH, INNER), BF16),
            pltpu.VMEM((2, WIDTH, 3 * WIDTH), BF16),
            pltpu.VMEM((2, WIDTH, WIDTH), BF16),
            pltpu.VMEM((2, WIDTH, INNER), BF16),
            pltpu.VMEM((2, INNER, WIDTH), BF16),
            pltpu.VMEM((WIDTH, 128), F32),
            pltpu.VMEM((16, SLOT), F32),
            pltpu.VMEM((8, SLOT), F32),
            pltpu.VMEM((WIDTH, SLOT), F32),
            parts(WIDTH),
            pltpu.VMEM((2, HEADS, 256, SLOT), BF16),
            pltpu.VMEM((2, HEADS, 256, SLOT), BF16),
            pltpu.VMEM((2, HEADS, 256, SLOT), BF16),
            parts(WIDTH),
            pltpu.VMEM((2, WIDTH, SLOT), F32),
            pltpu.VMEM((2, 1, SLOT), F32),
            parts(WIDTH),
            pltpu.VMEM((2, INNER, SLOT), F32),
            parts(INNER),
            pltpu.VMEM((2, WIDTH, SLOT), F32),
            pltpu.VMEM((2, 1, SLOT), F32),
            pltpu.VMEM((WIDTH, SLOT), F32),
            pltpu.VMEM((2, WIDTH, SLOT), BF16),
            pltpu.VMEM((2, INNER, SLOT), BF16),
            pltpu.VMEM((WIDTH, SLOT), F32),
            pltpu.VMEM((2, WIDTH, SLOT), BF16),
            pltpu.VMEM((HEADS, 256, SLOT), BF16),
            pltpu.VMEM((2 * HEAD, SLOT), F32),
            pltpu.VMEM((2, 3 * WIDTH, SLOT), BF16),
            pltpu.VMEM((10, WIDTH, 128), F32),
            pltpu.VMEM((2, PACKED_ROWS, WIDTH), F32),
            pltpu.SemaphoreType.DMA((10,)),
            pltpu.SemaphoreType.DMA((9,)),
            pltpu.SemaphoreType.DMA((9,)),
        ],
        compiler_params=pltpu.CompilerParams(
            collective_id=0, has_side_effects=True, vmem_limit_bytes=63 * 2 ** 20),
        name="relay",
    )(activations, cotangent, cell_lengths, w_qkv, w_out, w_in, w_back, vectors)


def sum_kernel(packed_ref, total_ref, small_ref, own, other, half_out, small_in, *scratch):
    (slots_x, slots_y, slots_z, sum_x, sum_y, small_slots, all_x, all_y, all_z, local_sem, send_sem, recv_sem) = scratch
    core = lax.axis_index("pipe")
    dp = lax.axis_index("dp")
    seq = lax.axis_index("seq")
    x_high, z, y = dp // 16, (dp // 4) % 4, dp % 4
    x = x_high * 2 + seq

    def at_x(index):
        return {"dp": (index // 2) * 16 + dp % 16, "seq": index % 2}

    def at_y(index):
        return {"dp": dp - y + index}

    def at_z(index):
        return {"dp": x_high * 16 + index * 4 + y}

    sibling = {"pipe": 1 - core}
    axes = ((at_x, x), (at_y, y), (at_z, z))

    barrier = pltpu.get_barrier_semaphore()
    pl.semaphore_signal(barrier, inc=1, device_id=sibling, device_id_type=MESH)
    for where, index in axes:
        for step in range(1, 4):
            pl.semaphore_signal(barrier, inc=1, device_id=where((index + step) % 4), device_id_type=MESH)
    pl.semaphore_wait(barrier, 10)

    used = [0]

    def remote(src, dst, device):
        index = used[0]
        used[0] += 1
        return pltpu.make_async_remote_copy(
            src_ref=src, dst_ref=dst, send_sem=send_sem.at[index], recv_sem=recv_sem.at[index],
            device_id=device, device_id_type=MESH,
        )

    rows = MATRIX_ROWS // 2
    sends = []
    for layer in range(2):
        sends.append(remote(
            packed_ref.at[layer, pl.ds(pl.multiple_of((1 - core) * rows, rows), rows)], other.at[layer], sibling))
    small_src = packed_ref.at[:, pl.ds(AT_SMALL, SMALL_ROWS)]
    sends.append(remote(small_src, small_slots.at[0, core], sibling))
    for copy in sends:
        copy.start()
    owns = [
        pltpu.make_async_copy(packed_ref.at[:, pl.ds(pl.multiple_of(core * rows, rows), rows)], own, local_sem.at[0]),
        pltpu.make_async_copy(small_src, small_slots.at[0, core], local_sem.at[1]),
    ]
    for copy in owns:
        copy.start()
    for copy in owns:
        copy.wait()
    for copy in sends:
        copy.wait()
    own[...] = own[...] + other[...]
    small_in[...] = small_slots[0, 0] + small_slots[0, 1]

    def chunk(ref, index, size):
        return ref.at[:, pl.ds(pl.multiple_of(index * size, size), size)]

    stages = (
        (axes[0], own, slots_x, sum_x, rows // 4),
        (axes[1], sum_x, slots_y, sum_y, rows // 16),
        (axes[2], sum_y, slots_z, None, rows // 64),
    )
    for number, ((where, index), source, slots, target, size) in enumerate(stages):
        sends = []
        small_slots[number + 1, index] = small_in[...]
        for step in range(1, 4):
            peer = (index + step) % 4
            sends.append(remote(chunk(source, peer, size), slots.at[index], where(peer)))
            sends.append(remote(small_in, small_slots.at[number + 1, index], where(peer)))
        for copy in sends:
            copy.start()
        slots[index] = source[:, pl.ds(pl.multiple_of(index * size, size), size)]
        for copy in sends:
            copy.wait()
        summed = (slots[0] + slots[1]) + (slots[2] + slots[3])
        small = (small_slots[number + 1, 0] + small_slots[number + 1, 1]) + (
            small_slots[number + 1, 2] + small_slots[number + 1, 3])
        small_in[...] = small
        if target is not None:
            target[...] = summed
        else:
            all_z[:, pl.ds(pl.multiple_of(index * size, size), size)] = summed

    whole = (all_x, all_y, all_z, None)
    for number, ((where, index), _, _, _, size) in reversed(list(enumerate(stages))):
        dest, source = whole[number], whole[number + 1]
        if source is not None:
            dest[:, pl.ds(pl.multiple_of(index * size, size), size)] = source[...]
        sends = []
        for step in range(1, 4):
            peer = (index + step) % 4
            sends.append(remote(chunk(dest, index, size), chunk(dest, index, size), where(peer)))
        for copy in sends:
            copy.start()
        for copy in sends:
            copy.wait()

    send = remote(all_x.at[1 - core], half_out, sibling)
    send.start()
    mine = pl.ds(pl.multiple_of(core * rows, rows), rows)
    theirs = pl.ds(pl.multiple_of((1 - core) * rows, rows), rows)
    keep = pltpu.make_async_copy(all_x.at[core], total_ref.at[mine], local_sem.at[2])
    keep.start()
    small_ref[...] = small_in[core]
    send.wait()
    last = pltpu.make_async_copy(half_out, total_ref.at[theirs], local_sem.at[3])
    last.start()
    keep.wait()
    last.wait()


def sum_grads(packed):
    rows = MATRIX_ROWS // 2
    count = 3 + 18 + 9 + 1
    return pl.pallas_call(
        sum_kernel,
        out_shape=(
            jax.ShapeDtypeStruct((MATRIX_ROWS, WIDTH), F32),
            jax.ShapeDtypeStruct((SMALL_ROWS, WIDTH), F32),
        ),
        in_specs=[pl.BlockSpec(memory_space=pl.ANY)],
        out_specs=(pl.BlockSpec(memory_space=pl.ANY), pl.BlockSpec(memory_space=pltpu.VMEM)),
        scratch_shapes=[
            pltpu.VMEM((2, rows, WIDTH), F32),
            pltpu.VMEM((2, rows, WIDTH), F32),
            pltpu.VMEM((rows, WIDTH), F32),
            pltpu.VMEM((2, SMALL_ROWS, WIDTH), F32),
            pltpu.VMEM((4, 2, rows // 4, WIDTH), F32),
            pltpu.VMEM((4, 2, rows // 16, WIDTH), F32),
            pltpu.VMEM((4, 2, rows // 64, WIDTH), F32),
            pltpu.VMEM((2, rows // 4, WIDTH), F32),
            pltpu.VMEM((2, rows // 16, WIDTH), F32),
            pltpu.VMEM((4, 4, 2, SMALL_ROWS, WIDTH), F32),
            pltpu.VMEM((2, rows, WIDTH), F32),
            pltpu.VMEM((2, rows // 4, WIDTH), F32),
            pltpu.VMEM((2, rows // 16, WIDTH), F32),
            pltpu.SemaphoreType.DMA((4,)),
            pltpu.SemaphoreType.DMA((count,)),
            pltpu.SemaphoreType.DMA((count,)),
        ],
        compiler_params=pltpu.CompilerParams(
            collective_id=1, has_side_effects=True, vmem_limit_bytes=48 * 2 ** 20),
        name="sum_grads",
    )(packed)


def body(
    activations, cotangent, cell_lengths, w_qkv, b_qv, w_out, b_out, gain_one, shift_one,
    w_in, b_in, w_back, b_back, gain_two, shift_two,
):
    vectors = jnp.concatenate(
        [b_qv, b_out, gain_one, shift_one, b_in, b_back, gain_two, shift_two, jnp.zeros((1, 6 * WIDTH), F32)], axis=1
    ).reshape(1, SMALL_ROWS, WIDTH)
    final_output, input_grad, packed = relay(
        activations, cotangent, cell_lengths, w_qkv, w_out, w_in, w_back, vectors)
    total, small = sum_grads(packed)

    def vector(first, count):
        return small[first:first + count].reshape(1, count * WIDTH)

    def matrix(first, count):
        blocks = [total[first + i * WIDTH:first + (i + 1) * WIDTH] for i in range(count)]
        return jnp.concatenate(blocks, axis=1)[None]

    return (
        final_output,
        input_grad,
        matrix(AT_QKV, 3),
        vector(V_Q, 2),
        matrix(AT_OUT, 1),
        vector(V_OUT, 1),
        vector(V_GAIN1, 1),
        vector(V_SHIFT1, 1),
        matrix(AT_IN, 2),
        vector(V_IN, 2),
        total[AT_BACK:AT_BACK + INNER][None],
        vector(V_BACK, 1),
        vector(V_GAIN2, 1),
        vector(V_SHIFT2, 1),
    )


def solution(mesh):
    rows = P(None, ("dp", "seq"), None)
    matrix = P("pipe", None, None)
    vector = P("pipe", None)
    in_specs = (
        rows, rows, P(None, "dp", None), matrix, vector, matrix, vector, vector, vector,
        matrix, vector, matrix, vector, vector, vector,
    )
    out_rows = P("pipe", ("dp", "seq"), None)
    out_specs = (
        out_rows, out_rows, matrix, vector, matrix, vector, vector, vector,
        matrix, vector, matrix, vector, vector, vector,
    )
    return jax.shard_map(body, mesh=mesh, in_specs=in_specs, out_specs=out_specs, check_vma=False)
```

time: 1360 us -> 217 us (0.16)
  matrix products: 541 us -> 0 us
  blocking collectives: 349 us -> 0 us
  waiting for transfers between devices: 212 us -> 0 us
  Pallas kernels: 0 us -> 200 us
  local copies, waits for them, and re-layouts: 140 us -> 12.9 us
  other arithmetic: 86.2 us -> 1.79 us
  between operations: 18 us -> 0.68 us
    dot_general x115 -> x0, matrix products: 541 us -> none  [the longest x10 98.4 us: head_scores(): jnp.einsum('qhd,khd->hqk', split_heads(queries), split_heads(key_rows), p...]
    psum x1 -> x0, blocking collectives: 349 us -> none  [reduce_grads(): lax.psum((grad_w_qkv, grad_b_qv, grad_w_out, grad_b_out, grad_gain_one, g...]
    pallas_call x0 -> x2, Pallas kernels: none -> 200 us  [the longest x1 113 us: relay(): pl.pallas_call(relay_kernel, out_shape=(shape((2, HALF, WIDTH), F32), sha...]
    all_gather x20 -> x0, waiting for transfers between devices: 180 us -> none  [the longest x5 100 us: layer_forward(): lax.all_gather(key_rows, 'seq', axis=0, tiled=True)]
    unnamed x371 -> x19, local copies, waits for them, and re-layouts: 64.3 us -> 10.5 us
    all_gather x20 -> x0, local copies, waits for them, and re-layouts: 51 us -> none  [the longest x5 13 us: layer_backward(): lax.all_gather(key_rows, 'seq', axis=0, tiled=True)]
    reduce_sum x66 -> x0, other arithmetic: 50.7 us -> none  [the longest x5 15.6 us: fold_keys(): row_total = jnp.sum(weights, axis=2)]
    reduce_scatter x10 -> x0, waiting for transfers between devices: 24.4 us -> none  [the longest x5 24.4 us: layer_backward(): lax.psum_scatter(grad_keys, 'seq', scatter_dimension=0, tiled=True)]
  transfers between devices with their start and end apart: 40 -> 0, of which waited for: 23 -> 0; matrix products, arithmetic and copies ran while one was open for 43% -> 0% of each run, Pallas kernels for 0% -> 0%
where the time goes in v1:
time: 217 us; the launch traced here: 216 us
  Pallas kernels  200 us (92%)
  local copies, waits for them, and re-layouts  12.9 us (6%)
    pallas_call x1, Pallas kernels, relay(): pl.pallas_call(relay_kernel, out_shape=(shape((2, HALF, WIDTH), F32), sha...  113 us
    pallas_call x1, Pallas kernels, sum_grads(): pl.pallas_call(sum_kernel, out_shape=(jax.ShapeDtypeStruct((MATRIX_ROWS,...  87.1 us
    unnamed x19, local copies, waits for them, and re-layouts  10.5 us

profile of v1, /device:TPU:0, one launch (start us, length us, event | category | flops | bytes accessed | tf_op | source)
XLA Modules:
  0.0 215.7 jit_solution(9613631951471304610)
XLA Ops:
  0.6 1.3 copy.29.len_ref
  2.0 0.7 constant_dynamic-update-slice_fusion.8
  2.7 0.7 constant_dynamic-update-slice_fusion.7
  3.4 0.7 constant_dynamic-update-slice_fusion.6
  4.0 0.7 constant_dynamic-update-slice_fusion.5
  4.7 0.7 constant_dynamic-update-slice_fusion.4
  5.4 0.7 constant_dynamic-update-slice_fusion.3
  6.1 0.7 constant_dynamic-update-slice_fusion.2
  6.8 0.7 constant_dynamic-update-slice_fusion.1
  7.5 0.6 copy.34
  8.1 113.3 %relay.1 = (f32[2,512,256]{2,1,0:T(8,128)}, f32[2,512,256]{2,1,0:T(8,128)}, f32[2,2064,256]{2,1,0:T(8,128)}) custom-call(f32[4,512,256]{2,1,0:T(8,128)} %act_ref.1, f32[4,512,256]{2,1,0:T(8,128)} %cot_ref.1, s32[4,1,3]{2,1,0:T(1,128)} %copy.29.len_ref, f32[1,256,768]{2,1,0:T(8,128)} %w_qkv_ref.1, f32[1,256,256]{2,1,0:T(8,128)} %w_out_ref.1, ...), custom_call_target="tpu_custom_call" | custom-call | tf_op jit(solution)/shard_map/relay/pallas_call | solution.py:395
  121.4 87.1 %sum_grads.1 = (f32[2048,256]{1,0:T(8,128)S(1)}, f32[16,256]{1,0:T(8,128)S(1)}) custom-call(f32[2,2064,256]{2,1,0:T(8,128)} %get-tuple-element.21.packed_ref), custom_call_target="tpu_custom_call" | custom-call | tf_op jit(solution)/shard_map/sum_grads/pallas_call | solution.py:575
  208.5 0.6 fusion.1
  209.1 0.6 copy.31
  209.6 0.6 copy.30
  210.2 0.8 slice_bitcast_fusion
  211.1 0.9 fusion
  211.9 0.0 copy-start.1
  211.9 0.9 maximum_bitcast_fusion.1
  212.8 0.0 copy-start
  212.8 0.9 maximum_bitcast_fusion
  213.7 0.0 copy-done.1
  213.7 1.0 copy.45
  214.7 0.0 copy-done
  214.7 1.0 copy.46
  (2 shorter events, 0.0 us)
Async XLA Ops:
  211.9 1.8 copy-start.1
  212.8 1.9 copy-start
